TPU v7x, 32 devices: a whole 2x2x4 slice. The times are simulated.
32 devices in a mesh: groups: 1, ctx: 16 (over z, y, x), exp: 2 (over core).
Axes of the slice: x: 2, y: 2, z: 4, core: 2. Of those that a mesh axis runs over, the one named last changes fastest.
Arguments:
- queries: bfloat16 [2048, 2048], P(('groups', 'ctx'), 'exp'), may hold values from -40 to 40
- key_rows: bfloat16 [2048, 256], P(('groups', 'ctx'), 'exp'), may hold values from -15 to 15
- value_rows: bfloat16 [2048, 256], P(('groups', 'ctx'), 'exp'), may hold values from -6 to 6
- hidden_in: bfloat16 [2048, 1024], P(('groups', 'ctx')), may hold values from -40 to 40
- out_proj: bfloat16 [2048, 1024], P('exp'), may hold values from -0.125 to 0.125
- norm_gain: float32 [1024], replicated, may hold values from 0.1 to 1.9
- expert_ids: int32 [2048, 8], P(('groups', 'ctx')), may hold values from 0 to 15, all different within a row; in each aligned block of 128 rows (0 to 127, 128 to 255, ...) at most 96 rows name the same one
- gate_scores: float32 [2048, 8], P(('groups', 'ctx')), may hold values from 0.05 to 1
- w_gate: bfloat16 [16, 1024, 384], P('ctx'), may hold values from -0.1875 to 0.1875
- w_up: bfloat16 [16, 1024, 384], P('ctx'), may hold values from -0.1875 to 0.1875
- w_down: bfloat16 [16, 384, 1024], P('ctx'), may hold values from -0.3125 to 0.3125
Outputs:
- layer_out: bfloat16 [2048, 1024], P(('groups', 'ctx'), 'exp')
Inputs may be any that keep to these rules, and one draw needn't show every extreme that they name: `expert_ids`: each row names 8 different experts. No expert is named by more than 96 rows of one aligned block of 128 rows, a bound that some block reaches.
All inputs are finite; a program needn't handle non-finite values.
Results may differ from a plain program's by a relative error of at most 0.0035.
Values may be sent and summed in bfloat16 or wider, within the bound.
A program may use at most 64 MiB of HBM per device.

v0:
```python
import math

import jax
import jax.numpy as jnp
from jax import lax
from jax.sharding import PartitionSpec as P


def attend(queries, key_rows, value_rows, first):
    token_count = queries.shape[0]
    kv_heads = key_rows.shape[1] // 128
    q_heads = queries.shape[1] // 128
    group = q_heads // kv_heads
    grouped = queries.reshape(token_count, kv_heads, group, 128)
    query_pos = first + jnp.arange(token_count, dtype=jnp.int32)
    last_pos = first + token_count - 1
    scale = 128 ** (-0.5)
    shape_rows = (kv_heads, group, token_count)
    start_state = (
        jnp.full(shape_rows, -1e30, jnp.float32),
        jnp.zeros(shape_rows, jnp.float32),
        jnp.zeros(shape_rows + (128,), jnp.float32),
    )
    key_piece = lax.all_gather(key_rows, "ctx", axis=0, tiled=True)
    value_piece = lax.all_gather(value_rows, "ctx", axis=0, tiled=True)
    count = key_piece.shape[0]
    width = math.gcd(count, 512)

    def step(block_index, state):
        offset = block_index * width

        def compute(inner):
            running_max, running_sum, accum = inner
            key_block = lax.dynamic_slice_in_dim(key_piece, block_index * width, width, 0).reshape(
                width, kv_heads, 128
            )
            value_block = lax.dynamic_slice_in_dim(
                value_piece, block_index * width, width, 0
            ).reshape(width, kv_heads, 128)
            scores = (
                jnp.einsum("tkgd,skd->kgts", grouped, key_block, preferred_element_type=jnp.float32)
                * scale
            )
            key_pos = offset + jnp.arange(width, dtype=jnp.int32)
            allowed = key_pos[None, :] <= query_pos[:, None]
            scores = jnp.where(allowed, scores, -jnp.inf)
            new_max = jnp.maximum(running_max, jnp.max(scores, axis=-1))
            factor = jnp.exp(running_max - new_max)
            weights = jnp.exp(scores - new_max[..., None])
            new_sum = running_sum * factor + jnp.sum(weights, axis=-1)
            product = jnp.einsum(
                "kgts,skd->kgtd",
                weights.astype(jnp.bfloat16),
                value_block,
                preferred_element_type=jnp.float32,
            )
            return (new_max, new_sum, accum * factor[..., None] + product)

        return lax.cond(offset <= last_pos, compute, lambda inner: inner, state)

    _, total, accum = lax.fori_loop(0, count // width, step, start_state)
    output = accum / total[..., None]
    return (
        jnp.transpose(output, (2, 0, 1, 3)).reshape(token_count, q_heads * 128).astype(jnp.bfloat16)
    )


def place_rows(expert_ids, sent_rows, capacity, expert_count):
    top_count = expert_ids.shape[1]
    flat_ids = expert_ids.reshape(-1)
    onehot = (flat_ids[:, None] == jnp.arange(expert_count, dtype=jnp.int32)[None, :]).astype(
        jnp.int32
    )
    earlier = jnp.cumsum(onehot, axis=0) - onehot
    slot_index = jnp.sum(earlier * onehot, axis=1)
    destination = flat_ids * capacity + slot_index
    copies = jnp.repeat(sent_rows, top_count, axis=0)
    buffer = (
        jnp.zeros((expert_count * capacity, sent_rows.shape[1]), sent_rows.dtype)
        .at[destination]
        .set(copies)
    )
    return (buffer.reshape(expert_count, 2, capacity // 2, sent_rows.shape[1]), destination)


def per_device(
    queries,
    key_rows,
    value_rows,
    hidden_in,
    out_proj,
    norm_gain,
    expert_ids,
    gate_scores,
    w_gate,
    w_up,
    w_down,
):
    token_count = queries.shape[0]
    model_width = hidden_in.shape[1]
    half_width = model_width // 2
    ctx_size = lax.axis_size("ctx")
    local_experts = w_gate.shape[0]
    expert_count = local_experts * ctx_size
    top_count = expert_ids.shape[1]
    capacity = 2 * (
        min(token_count, max(2, 3 * token_count * top_count // (2 * expert_count))) // 2
    )
    half_cap = capacity // 2
    first = lax.axis_index("ctx") * token_count
    core = lax.axis_index("exp")
    side_start = core * half_width
    attended = attend(queries, key_rows, value_rows, first)
    head_part = jnp.dot(attended, out_proj, preferred_element_type=jnp.float32)
    attn_full = lax.psum(head_part.astype(jnp.bfloat16), "exp").astype(jnp.float32)
    resid = hidden_in.astype(jnp.float32) + attn_full
    inverse = lax.rsqrt(jnp.mean(resid * resid, axis=1, keepdims=True) + 1e-06)
    sent_rows = (resid * inverse * norm_gain[None, :]).astype(jnp.bfloat16)
    resid_half = lax.dynamic_slice_in_dim(resid, side_start, half_width, 1)
    buffer, destination = place_rows(expert_ids, sent_rows, capacity, expert_count)
    own_slots = lax.dynamic_slice_in_dim(buffer, core, 1, 1)
    grouped = lax.all_to_all(own_slots, "ctx", split_axis=0, concat_axis=0, tiled=True)
    gate = jnp.einsum("sxmd,xdf->sxmf", grouped, w_gate, preferred_element_type=jnp.float32)
    upper = jnp.einsum("sxmd,xdf->sxmf", grouped, w_up, preferred_element_type=jnp.float32)
    hidden = (jax.nn.silu(gate) * upper).astype(jnp.bfloat16)
    partial_value = jnp.einsum(
        "sxmf,xfd->sxmd", hidden, w_down, preferred_element_type=jnp.float32
    ).astype(jnp.bfloat16)
    returned = lax.all_to_all(partial_value, "ctx", split_axis=0, concat_axis=0, tiled=True)
    flat_back = returned.reshape(expert_count * half_cap, model_width)
    slot_of = destination % capacity
    expert_of = destination // capacity
    owned = slot_of // half_cap == core
    local_index = jnp.where(owned, expert_of * half_cap + slot_of - core * half_cap, 0)
    picked = flat_back[local_index].astype(jnp.float32)
    mixing = (gate_scores / jnp.sum(gate_scores, axis=1, keepdims=True)).reshape(-1)
    mixing = jnp.where(owned, mixing, 0.0)
    weighted = (picked * mixing[:, None]).reshape(token_count, top_count, model_width)
    mixed_part = jnp.sum(weighted, axis=1)
    moe_half = lax.psum_scatter(
        mixed_part.astype(jnp.bfloat16), "exp", scatter_dimension=1, tiled=True
    ).astype(jnp.float32)
    return (resid_half + moe_half).astype(jnp.bfloat16)


def solution(mesh):
    placed = (
        P(("groups", "ctx"), "exp"),
        P(("groups", "ctx"), "exp"),
        P(("groups", "ctx"), "exp"),
        P(("groups", "ctx"), None),
        P("exp", None),
        P(),
        P(("groups", "ctx"), None),
        P(("groups", "ctx"), None),
        P("ctx", None, None),
        P("ctx", None, None),
        P("ctx", None, None),
    )
    return jax.shard_map(
        per_device,
        mesh=mesh,
        in_specs=placed,
        out_specs=P(("groups", "ctx"), "exp"),
        check_vma=False,
    )
```

profile of v0, /device:TPU:0, one launch (start us, length us, event | category | flops | bytes accessed | tf_op | source)
XLA Modules:
  0.0 254.6 jit_solution(11516045207703964452)
XLA Ops:
  6.5 45.7 %all_gather.6 = bf16[2048,128]{1,0:T(8,128)(2,1)S(1)} all-gather(bf16[128,128]{1,0:T(8,128)(2,1)} %param.16), channel_id=1, replica_groups=mesh['groups'=1,'ctx'=16,'exp'=2] {'ctx'}, dimensions={0}, use_global_device_ids=true | all-gather | bytes 557056 | tf_op jit(solution)/shard_map/all_gather | solution.py:24
  52.3 41.0 %all_gather.7 = bf16[2048,128]{1,0:T(8,128)(2,1)} all-gather(bf16[128,128]{1,0:T(8,128)(2,1)} %param.17), channel_id=1, replica_groups=mesh['groups'=1,'ctx'=16,'exp'=2] {'ctx'}, dimensions={0}, use_global_device_ids=true | all-gather | bytes 557056 | tf_op jit(solution)/shard_map/all_gather | solution.py:25
  93.2 1.1 copy.47
  94.6 2.8 %while.18 = (s32[]{:T(128)}, f32[1,8,128]{2,1,0:T(8,128)S(1)}, f32[1,8,128]{2,1,0:T(8,128)S(1)}, f32[1,8,128,128]{3,2,1,0:T(8,128)S(1)}, s32[]{:T(128)}, /*index...) while((s32[]{:T(128)}, f32[1,8,128]{2,1,0:T(8,128)S(1)}, ...), condition=%wide.region_5.6_spmd.clone, body=%wide.region_0.5_spmd.clone.sunk | while | flops 272436864 | bytes 8067405 | solution.py:61
  94.6 2.6 %conditional.3 = ((f32[1,8,128]{2,1,0:T(8,128)S(1)}, f32[1,8,128]{2,1,0:T(8,128)S(1)}, f32[1,8,128,128]{3,2,1,0:T(8,128)S(1)})) conditional(s32[]{:T(128)} %convert_element_type.120, (f32[1,8,128]{2,1,0:T(8,128)S(1)}, f32[1,8,128]{2,1,0:T(8,128)S(1)}, f32[1,8,128,128]{3,2,1,0:T(8,128)S(1)}) %tuple.49, (s32[]{:T(128)}, s32[]{:T(128)}, s32[]{:T(128)}, ...), branch_computations={%region_1.0_spmd, %region_2.4_spmd} | conditional | flops 272436864 | bytes 8066654 | solution.py:59
  94.8 0.4 fusion.55
  95.3 1.6 fusion.4
  97.7 1.2 convolution_convert_fusion.1
  99.3 4.5 %reduce-window.6 = s32[16,8,128]{2,1,0:T(8,128)S(1)} reduce-window(s32[16,8,128]{2,1,0:T(8,128)S(1)} %fusion.51, s32[]{:T(128)} %constant.82.clone.1), window={size=1x1x128 pad=0_0x0_0x127_0}, to_apply=%region_7.8 | reduce-window | flops 2080768 | bytes 131076 | tf_op jit(solution)/shard_map/reduce-window
  104.5 18.7 %all-reduce.2.cloned.1.call-done = bf16[128,1024]{1,0:T(8,128)(2,1)} async-done(((bf16[128,1024]{1,0:T(8,128)(2,1)}), bf16[128,1024]{1,0:T(8,128)(2,1)}) %all-reduce.2.cloned.1.call-update) | async-done | bytes 262160 | tf_op jit(solution)/shard_map/psum | solution.py:115
  123.2 1.1 convert_add_fusion
  124.4 1.1 multiply_convert_fusion
  125.4 7.4 %scatter_custom_fusion = bf16[1536,1024]{1,0:T(8,128)(2,1)} fusion(s32[1024]{0:T(1024)S(1)} %bitcast.140, bf16[]{:T(256)} %constant.91.clone.1, bf16[128,1024]{1,0:T(8,128)(2,1)S(1)} %multiply_convert_fusion), kind=kCustom, calls=%fused_computation.27 | custom fusion | bytes 3407874 | tf_op jit(solution)/shard_map/scatter | solution.py:81
  132.8 1.6 constant_dynamic-slice_fusion
  134.4 44.7 %all_to_all.10 = bf16[16,1,48,1024]{3,2,1,0:T(8,128)(2,1)S(1)} all-to-all(bf16[16,1,48,1024]{3,2,1,0:T(8,128)(2,1)S(1)} %constant_dynamic-slice_fusion), channel_id=1, replica_groups=mesh['groups'=1,'ctx'=16,'exp'=2] {'ctx'}, dimensions={0} | all-to-all | bytes 3145728 | tf_op jit(solution)/shard_map/all_to_all | solution.py:122
  179.1 1.1 copy-done.1
  180.2 2.0 fusion.25
  182.2 5.2 %fusion.24 = bf16[16,1,48,1024]{3,2,1,0:T(8,128)(2,1)} fusion(bf16[16,1,48,1024]{3,2,1,0:T(8,128)(2,1)} %copy-done.1, f32[16,1,48,384]{3,2,0,1:T(8,128)} %fusion.25, bf16[1,384,1024]{2,1,0:T(8,128)(2,1)} %param.25, bf16[1,1024,384]{2,1,0:T(8,128)(2,1)} %param.24), kind=kOutput, calls=%fused_computation.35 | convolution fusion | flops 1210515456 | bytes 5898240 | tf_op jit(solution)/shard_map/sxmf,xfd->sxmd/dot_general | solution.py:126
  187.4 4.5 %all-to-all-start.1 = ((bf16[16,1,48,1024]{3,2,1,0:T(8,128)(2,1)}), bf16[16,1,48,1024]{3,2,1,0:T(8,128)(2,1)}, u32[]{:S(2)}, u32[]{:S(2)}) async-start(bf16[16,1,48,1024]{3,2,1,0:T(8,128)(2,1)} %fusion.24), calls=%async_computation.1 | async-start | bytes 3145728 | tf_op jit(solution)/shard_map/all_to_all | solution.py:129
  192.5 32.8 %all-to-all-done.1 = bf16[16,1,48,1024]{3,2,1,0:T(8,128)(2,1)} async-done(((bf16[16,1,48,1024]{3,2,1,0:T(8,128)(2,1)}), bf16[16,1,48,1024]{3,2,1,0:T(8,128)(2,1)}, u32[]{:S(2)}, u32[]{:S(2)}) %all-to-all-start.1) | async-done | bytes 1572896 | tf_op jit(solution)/shard_map/all_to_all | solution.py:129
  225.3 7.6 %gather_fusion = bf16[1024,1024]{1,0:T(8,128)(2,1)} fusion(bf16[768,1024]{1,0:T(8,128)(2,1)} %bitcast.41, s32[1024]{0:T(1024)S(1)} %broadcast_clamp_fusion), kind=kCustom, calls=%fused_computation | custom fusion | bytes 4198400 | tf_op jit(solution)/shard_map/gather | solution.py:135
  233.0 3.7 %fusion.16 = bf16[128,1024]{1,0:T(8,128)(2,1)} fusion(bf16[1024,1024]{1,0:T(8,128)(2,1)} %gather_fusion, f32[128,8]{1,0:T(8,128)S(1)} %copy.57), kind=kLoop, calls=%fused_computation.26 | loop fusion | flops 3014656 | bytes 2363392 | tf_op jit(solution)/shard_map/reduce_sum | solution.py:139
  236.7 9.5 %reduce-scatter.2.cloned.1.call-done = bf16[128,512]{1,0:T(8,128)(2,1)} async-done(((bf16[128,1024]{1,0:T(8,128)(2,1)}), bf16[128,512]{1,0:T(8,128)(2,1)}) %reduce-scatter.2.cloned.1.call-update) | async-done | bytes 131088 | tf_op jit(solution)/shard_map/reduce_scatter | solution.py:140
  246.2 1.6 add_convert_fusion
  (59 shorter events, 2.6 us)
Async XLA Ops:
  6.5 91.2 %copy-start = (bf16[1024,1024]{1,0:T(8,128)(2,1)S(1)}, bf16[1024,1024]{1,0:T(8,128)(2,1)}, u32[]{:S(2)}) copy-start(bf16[1024,1024]{1,0:T(8,128)(2,1)} %param.19) | copy-start | bytes 6291460
  6.5 116.7 %all-reduce.2.cloned.1.call-start = ((), (), s32[]{:S(2)}) async-start(), calls=%async_computation.3 | async-start | bytes 524288 | tf_op jit(solution)/shard_map/psum | solution.py:115
  97.6 1.3 copy-start.3
  97.7 25.5 %copy-start.2 = (bf16[128,1024]{1,0:T(8,128)(2,1)S(1)}, bf16[128,1024]{1,0:T(8,128)(2,1)}, u32[]{:S(2)}) copy-start(bf16[128,1024]{1,0:T(8,128)(2,1)} %param.18) | copy-start | bytes 786436
  97.7 26.6 %copy-start.5 = (f32[1024]{0:T(1024)S(1)}, f32[1024]{0:T(1024)}, u32[]{:S(2)}) copy-start(f32[1024]{0:T(1024)} %param.20) | copy-start | bytes 12292
  134.4 45.8 %copy-start.6 = (bf16[1,1024,384]{2,1,0:T(8,128)(2,1)S(1)}, bf16[1,1024,384]{2,1,0:T(8,128)(2,1)}, u32[]{:S(2)}) copy-start(bf16[1,1024,384]{2,1,0:T(8,128)(2,1)} %param.23) | copy-start | bytes 2359300
  179.1 1.1 copy-start.1
  187.4 4.9 %copy-start.4 = (f32[128,8]{0,1:T(8,128)S(1)}, f32[128,8]{0,1:T(8,128)}, u32[]{:S(2)}) copy-start(f32[128,8]{0,1:T(8,128)} %param.22) | copy-start | bytes 12292
  187.4 37.9 %all-to-all-start.1 = ((bf16[16,1,48,1024]{3,2,1,0:T(8,128)(2,1)}), bf16[16,1,48,1024]{3,2,1,0:T(8,128)(2,1)}, u32[]{:S(2)}, u32[]{:S(2)}) async-start(bf16[16,1,48,1024]{3,2,1,0:T(8,128)(2,1)} %fusion.24), calls=%async_computation.1 | async-start | bytes 3145728 | tf_op jit(solution)/shard_map/all_to_all | solution.py:129
  191.9 54.2 %reduce-scatter.2.cloned.1.call-start = ((), (), s32[]{:S(2)}) async-start(), calls=%async_computation.4 | async-start | bytes 393216 | tf_op jit(solution)/shard_map/reduce_scatter | solution.py:140
Sparse Core Ops, SparseCore 0:
  99.1 24.1 all-reduce.1
  236.8 9.3 reduce-scatter.1
where the time goes:
time: 255 us
  blocking collectives  131 us (51%)
  waiting for transfers between devices  61.1 us (24%)
  local copies, waits for them, and re-layouts  20.3 us (8%)
  between operations  13.6 us (5%)
  other arithmetic  12.8 us (5%)
  matrix products  10.4 us (4%)
  starting transfers between devices  4.76 us (2%)
    all_gather x1, blocking collectives, attend(): key_piece = lax.all_gather(key_rows, 'ctx', axis=0, tiled=True)  45.7 us
    all_to_all x1, blocking collectives, per_device(): lax.all_to_all(own_slots, 'ctx', split_axis=0, concat_axis=0, tiled=True)  44.7 us
    all_gather x1, blocking collectives, attend(): value_piece = lax.all_gather(value_rows, 'ctx', axis=0, tiled=True)  41 us
    all_to_all x1, waiting for transfers between devices, per_device(): lax.all_to_all(partial_value, 'ctx', split_axis=0, concat_axis=0, tiled=T...  32.8 us
    psum x1, waiting for transfers between devices, per_device(): lax.psum(head_part.astype(jnp.bfloat16), 'exp').astype(jnp.float32)  18.7 us
    reduce_scatter x1, waiting for transfers between devices, per_device(): lax.psum_scatter(mixed_part.astype(jnp.bfloat16), 'exp', scatter_dimensio...  9.5 us
    gather x1, local copies, waits for them, and re-layouts, per_device(): picked = flat_back[local_index].astype(jnp.float32)  7.65 us
    scatter x1, local copies, waits for them, and re-layouts, place_rows(): buffer = jnp.zeros((expert_count * capacity, sent_rows.shape[1]), sent_ro...  7.39 us
  transfers between devices with their start and end apart: 3, of which 3 were waited for; matrix products, arithmetic and copies ran while one was open for 2% of the time, Pallas kernels for 0%

commit v1 on v0

--- a/solution.py
+++ b/solution.py
@@ -1,9 +1,18 @@
+import functools
 import math
 
 import jax
 import jax.numpy as jnp
 from jax import lax
+from jax.experimental import pallas as pl
+from jax.experimental.pallas import tpu as pltpu
 from jax.sharding import PartitionSpec as P
+
+MESH = pl.DeviceIdType.MESH
+HEAD = 128
+PIECES = 2
+NEG = -1e30
+STAGGER = 1
 
 
 def attend(queries, key_rows, value_rows, first):
@@ -71,7 +80,11 @@
     onehot = (flat_ids[:, None] == jnp.arange(expert_count, dtype=jnp.int32)[None, :]).astype(
         jnp.int32
     )
-    earlier = jnp.cumsum(onehot, axis=0) - onehot
+    index = jnp.arange(flat_ids.shape[0], dtype=jnp.int32)
+    before = (index[None, :] < index[:, None]).astype(jnp.bfloat16)
+    earlier = jnp.dot(
+        before, onehot.astype(jnp.bfloat16), preferred_element_type=jnp.float32
+    ).astype(jnp.int32)
     slot_index = jnp.sum(earlier * onehot, axis=1)
     destination = flat_ids * capacity + slot_index
     copies = jnp.repeat(sent_rows, top_count, axis=0)
@@ -143,6 +156,393 @@
     return (resid_half + moe_half).astype(jnp.bfloat16)
 
 
+def layer_kernel(
+    n,
+    q_ref,
+    k_ref,
+    v_ref,
+    hid_ref,
+    proj_hbm,
+    gain_ref,
+    ids_ref,
+    gate_ref,
+    wg_hbm,
+    wu_hbm,
+    wd_hbm,
+    out_ref,
+    kv_buf,
+    co_buf,
+    row_buf,
+    con_buf,
+    rs_bufs,
+    half_out,
+    half_in,
+    fin_out,
+    fin_in,
+    queries,
+    top,
+    den,
+    acc,
+    att,
+    resid,
+    by_token,
+    proj,
+    wg,
+    wu,
+    wd,
+    load_sem,
+    kv_sem,
+    co_sem,
+    ag_sem,
+    rs_sem,
+    half_sem,
+    fin_sem,
+):
+    me = lax.axis_index("ctx")
+    core = lax.axis_index("exp")
+    group = lax.axis_index("groups")
+    bits = n.bit_length() - 1
+    rows = q_ref.shape[0]
+    heads = q_ref.shape[1] // HEAD
+    half = rows // 2
+    piece_rows = half // PIECES
+    width = hid_ref.shape[1]
+    side = width // 2
+    coord = [(me // 2 ** (bits - 1 - d)) % 2 for d in range(bits)]
+    partner = [me + (1 - 2 * coord[d]) * 2 ** (bits - 1 - d) for d in range(bits)]
+    forward = list(range(bits))
+    crossed = forward[:-2] + [forward[-1], forward[-2]]
+    orders = [forward if p % 2 == 0 else crossed for p in range(PIECES)]
+    other = 1 - core
+
+    loads = [
+        pltpu.make_async_copy(src, dst, load_sem.at[i])
+        for i, (src, dst) in enumerate(
+            [(proj_hbm, proj), (wg_hbm.at[0], wg), (wu_hbm.at[0], wu), (wd_hbm.at[0], wd)]
+        )
+    ]
+    for load in loads:
+        load.start()
+
+    barrier = pltpu.get_barrier_semaphore()
+    for d in range(bits):
+        pl.semaphore_signal(
+            barrier, inc=1, device_id=(group, partner[d], core), device_id_type=MESH
+        )
+    pl.semaphore_signal(barrier, inc=1, device_id=(group, me, other), device_id_type=MESH)
+
+    own = tuple(coord)
+    kv_buf[(0,) + own] = k_ref[...]
+    kv_buf[(1,) + own] = v_ref[...]
+    mix = gate_ref[...] / jnp.sum(gate_ref[...], axis=1, keepdims=True)
+    lane = lax.broadcasted_iota(jnp.int32, (rows, HEAD), 1)
+    coef = jnp.zeros((rows, HEAD), jnp.float32)
+    for k in range(ids_ref.shape[1]):
+        coef = coef + jnp.where(ids_ref[:, k : k + 1] == lane, mix[:, k : k + 1], 0.0)
+    co_buf[own] = coef.T[: co_buf.shape[bits]]
+    pl.semaphore_wait(barrier, bits + 1)
+
+    def gather(buf, lead, order, step, sems):
+        done = order[:step]
+        where = lead + tuple(slice(None) if d in done else coord[d] for d in range(bits))
+        return pltpu.make_async_remote_copy(
+            src_ref=buf.at[where],
+            dst_ref=buf.at[where],
+            send_sem=sems[0],
+            recv_sem=sems[1],
+            device_id=(group, partner[order[step]], core),
+            device_id_type=MESH,
+        )
+
+    sent = []
+
+    def kv_copies(step):
+        copies = [
+            gather(
+                kv_buf,
+                (i,),
+                [forward, crossed][i],
+                step,
+                (kv_sem.at[i, step, 0], kv_sem.at[i, step, 1]),
+            )
+            for i in range(2)
+        ]
+        copies.append(
+            gather(co_buf, (), forward, step, (co_sem.at[step, 0], co_sem.at[step, 1]))
+        )
+        return copies
+
+    for step in range(bits):
+        copies = kv_copies(step)
+        for copy in copies:
+            copy.start()
+        if step == 0:
+            for h in range(heads):
+                queries[h] = q_ref[:, h * HEAD : (h + 1) * HEAD]
+            top[...] = jnp.full(top.shape, NEG, jnp.float32)
+            den[...] = jnp.zeros(den.shape, jnp.float32)
+            acc[...] = jnp.zeros(acc.shape, jnp.float32)
+        for copy in copies:
+            copy.wait_recv()
+        sent += copies
+
+    span = 4 * rows
+    chunk = me // 4
+    unit = HEAD ** (-0.5) * math.log2(math.e)
+    row_pos = lax.broadcasted_iota(jnp.int32, (rows, span), 0) + (me % 4) * rows
+    col_pos = lax.broadcasted_iota(jnp.int32, (rows, span), 1)
+
+    def attend_chunk(j, carry):
+        at = tuple((j // 2 ** (bits - 3 - d)) % 2 for d in range(bits - 2))
+        keys = kv_buf[(0,) + at].reshape(span, HEAD)
+        values = kv_buf[(1,) + at].reshape(span, HEAD)
+        allowed = col_pos <= row_pos + (chunk - j) * span
+        for h in range(heads):
+            scores = lax.dot_general(
+                queries[h], keys, (((1,), (1,)), ((), ())), preferred_element_type=jnp.float32
+            )
+            scores = jnp.where(allowed, scores, NEG)
+            old = top[h][:, :1]
+            new = jnp.maximum(old, jnp.max(scores, axis=1, keepdims=True))
+            factor = jnp.exp2((old - new) * unit)
+            weights = jnp.exp2((scores - new) * unit)
+            total = den[h][:, :1] * factor + jnp.sum(weights, axis=1, keepdims=True)
+            product = jnp.dot(
+                weights.astype(jnp.bfloat16), values, preferred_element_type=jnp.float32
+            )
+            acc[h] = acc[h] * factor + product
+            top[h] = jnp.broadcast_to(new, (rows, HEAD))
+            den[h] = jnp.broadcast_to(total, (rows, HEAD))
+        return carry
+
+    lax.fori_loop(0, chunk + 1, attend_chunk, 0)
+    for h in range(heads):
+        att[:, h * HEAD : (h + 1) * HEAD] = (acc[h] / den[h]).astype(jnp.bfloat16)
+
+    loads[0].wait()
+    mine = pl.ds(pl.multiple_of(core * half, half), half)
+    theirs = pl.ds(pl.multiple_of(other * half, half), half)
+    half_out[...] = jnp.dot(
+        att[theirs, :], proj[...], preferred_element_type=jnp.float32
+    ).astype(jnp.bfloat16)
+    swap = pltpu.make_async_remote_copy(
+        src_ref=half_out,
+        dst_ref=half_in,
+        send_sem=half_sem.at[0],
+        recv_sem=half_sem.at[1],
+        device_id=(group, me, other),
+        device_id_type=MESH,
+    )
+    swap.start()
+    resid[...] = hid_ref[mine, :].astype(jnp.float32) + jnp.dot(
+        att[mine, :], proj[...], preferred_element_type=jnp.float32
+    )
+    by_token[...] = jnp.zeros(by_token.shape, jnp.float32)
+    for b in range(n):
+        at = tuple((b // 2 ** (bits - 1 - d)) % 2 for d in range(bits))
+        by_token[b : b + 1, :] = co_buf[at + (pl.ds(me, 1), slice(None))]
+    by_token[...] = by_token[...].T
+    swap.wait_recv()
+    sent.append(swap)
+    full = resid[...] + half_in[...].astype(jnp.float32)
+    resid[...] = full
+    inverse = lax.rsqrt(jnp.mean(full * full, axis=1, keepdims=True) + 1e-06)
+    normed = (full * inverse * gain_ref[...]).astype(jnp.bfloat16)
+
+    def row_copy(p, step):
+        return gather(
+            row_buf, (p,), orders[p], step, (ag_sem.at[p, step, 0], ag_sem.at[p, step, 1])
+        )
+
+    def rs_copy(p, step):
+        order = orders[p][::-1]
+        done = order[:step]
+        turn = order[step]
+        where = (p,) + tuple(
+            coord[d] if d in done else (1 - coord[d] if d == turn else slice(None))
+            for d in range(bits)
+        )
+        return pltpu.make_async_remote_copy(
+            src_ref=con_buf.at[where],
+            dst_ref=rs_bufs[step].at[p],
+            send_sem=rs_sem.at[p, step, 0],
+            recv_sem=rs_sem.at[p, step, 1],
+            device_id=(group, partner[turn], core),
+            device_id_type=MESH,
+        )
+
+    def fin_copy(p):
+        return pltpu.make_async_remote_copy(
+            src_ref=fin_out.at[p],
+            dst_ref=fin_in.at[p],
+            send_sem=fin_sem.at[p, 0],
+            recv_sem=fin_sem.at[p, 1],
+            device_id=(group, me, other),
+            device_id_type=MESH,
+        )
+
+    def experts(p):
+        if p == 0:
+            for load in loads[1:]:
+                load.wait()
+        count = n * piece_rows
+        x = row_buf[p].reshape(count, width)
+        gate = jnp.dot(x, wg[...], preferred_element_type=jnp.float32)
+        upper = jnp.dot(x, wu[...], preferred_element_type=jnp.float32)
+        hidden = (gate / (1.0 + jnp.exp(-gate)) * upper).astype(jnp.bfloat16)
+        part = jnp.dot(hidden, wd[...], preferred_element_type=jnp.float32)
+        first = pl.multiple_of(core * half + p * piece_rows, piece_rows)
+        columns = by_token[pl.ds(first, piece_rows), :]
+        for b in range(n):
+            at = tuple((b // 2 ** (bits - 1 - d)) % 2 for d in range(bits))
+            con_buf[(p,) + at] = (
+                part[b * piece_rows : (b + 1) * piece_rows] * columns[:, b : b + 1]
+            ).astype(jnp.bfloat16)
+
+    def stage(p, s):
+        if s == 0:
+            row_buf[(p,) + own] = normed[p * piece_rows : (p + 1) * piece_rows]
+            row_copy(p, 0).start()
+            return
+        if s <= bits:
+            copy = row_copy(p, s - 1)
+            copy.wait_recv()
+            sent.append(copy)
+            if s < bits:
+                row_copy(p, s).start()
+                return
+            experts(p)
+            rs_copy(p, 0).start()
+            return
+        s -= bits + 1
+        if s < bits:
+            copy = rs_copy(p, s)
+            copy.wait_recv()
+            sent.append(copy)
+            order = orders[p][::-1]
+            where = (p,) + tuple(
+                coord[d] if d in order[: s + 1] else slice(None) for d in range(bits)
+            )
+            total = con_buf[where].astype(jnp.float32) + rs_bufs[s][p].astype(jnp.float32)
+            if s < bits - 1:
+                con_buf[where] = total.astype(jnp.bfloat16)
+                rs_copy(p, s + 1).start()
+                return
+            result = resid[p * piece_rows : (p + 1) * piece_rows] + total
+            result = result.astype(jnp.bfloat16)
+            left, right = result[:, :side], result[:, side:]
+            fin_out[p] = jnp.where(core == 0, right, left)
+            fin_copy(p).start()
+            first = pl.multiple_of(core * half + p * piece_rows, piece_rows)
+            out_ref[pl.ds(first, piece_rows), :] = jnp.where(core == 0, left, right)
+            return
+        copy = fin_copy(p)
+        copy.wait_recv()
+        sent.append(copy)
+        first = pl.multiple_of(other * half + p * piece_rows, piece_rows)
+        out_ref[pl.ds(first, piece_rows), :] = fin_in[p]
+
+    stages = 2 * bits + 2
+    plan = sorted((s + STAGGER * p, p, s) for p in range(PIECES) for s in range(stages))
+    for _, p, s in plan:
+        stage(p, s)
+    for copy in sent:
+        copy.wait_send()
+
+
+def fused_layer(n, *args):
+    queries, key_rows, value_rows, hidden_in, out_proj = args[:5]
+    norm_gain, expert_ids, gate_scores, w_gate, w_up, w_down = args[5:]
+    rows, width = hidden_in.shape
+    heads = queries.shape[1] // HEAD
+    bits = n.bit_length() - 1
+    half = rows // 2
+    piece_rows = half // PIECES
+    cube = (2,) * bits
+    vmem = pl.BlockSpec(memory_space=pltpu.VMEM)
+    anywhere = pl.BlockSpec(memory_space=pl.ANY)
+    bf16, f32 = jnp.bfloat16, jnp.float32
+    scratch = [
+        pltpu.VMEM((2,) + cube + (rows, HEAD), bf16),
+        pltpu.VMEM(cube + (-(-n // 8) * 8, rows), f32),
+        pltpu.VMEM((PIECES,) + cube + (piece_rows, width), bf16),
+        pltpu.VMEM((PIECES,) + cube + (piece_rows, width), bf16),
+        [
+            pltpu.VMEM((PIECES,) + cube[s + 1 :] + (piece_rows, width), bf16)
+            for s in range(bits)
+        ],
+        pltpu.VMEM((half, width), bf16),
+        pltpu.VMEM((half, width), bf16),
+        pltpu.VMEM((PIECES, piece_rows, width // 2), bf16),
+        pltpu.VMEM((PIECES, piece_rows, width // 2), bf16),
+        pltpu.VMEM((heads, rows, HEAD), bf16),
+        pltpu.VMEM((heads, rows, HEAD), f32),
+        pltpu.VMEM((heads, rows, HEAD), f32),
+        pltpu.VMEM((heads, rows, HEAD), f32),
+        pltpu.VMEM((rows, heads * HEAD), bf16),
+        pltpu.VMEM((half, width), f32),
+        pltpu.VMEM((rows, rows), f32),
+        pltpu.VMEM(out_proj.shape, bf16),
+        pltpu.VMEM(w_gate.shape[1:], bf16),
+        pltpu.VMEM(w_up.shape[1:], bf16),
+        pltpu.VMEM(w_down.shape[1:], bf16),
+        pltpu.SemaphoreType.DMA((4,)),
+        pltpu.SemaphoreType.DMA((2, bits, 2)),
+        pltpu.SemaphoreType.DMA((bits, 2)),
+        pltpu.SemaphoreType.DMA((PIECES, bits, 2)),
+        pltpu.SemaphoreType.DMA((PIECES, bits, 2)),
+        pltpu.SemaphoreType.DMA((2,)),
+        pltpu.SemaphoreType.DMA((PIECES, 2)),
+    ]
+    return pl.pallas_call(
+        functools.partial(layer_kernel, n),
+        out_shape=jax.ShapeDtypeStruct((rows, width // 2), bf16),
+        in_specs=[vmem] * 4 + [anywhere] + [vmem] * 3 + [anywhere] * 3,
+        out_specs=vmem,
+        scratch_shapes=scratch,
+        compiler_params=pltpu.CompilerParams(
+            collective_id=0, has_side_effects=True, vmem_limit_bytes=48 * 2**20
+        ),
+    )(
+        queries,
+        key_rows,
+        value_rows,
+        hidden_in,
+        out_proj,
+        norm_gain.reshape(1, width),
+        expert_ids,
+        gate_scores,
+        w_gate,
+        w_up,
+        w_down,
+    )
+
+
+def fits_fused(n, cores, args):
+    queries, key_rows, hidden_in = args[0], args[1], args[3]
+    expert_ids, w_gate = args[6], args[8]
+    rows, width = hidden_in.shape
+    return (
+        cores == 2
+        and n >= 8
+        and n & (n - 1) == 0
+        and n <= HEAD
+        and w_gate.shape[0] == 1
+        and 2 * expert_ids.shape[1] >= n
+        and key_rows.shape[1] == HEAD
+        and rows == HEAD
+        and width % (2 * HEAD) == 0
+        and n * rows * width * 2 <= 8 * 2**20
+    )
+
+
+def layer(*args):
+    n, cores = lax.axis_size("ctx"), lax.axis_size("exp")
+    if fits_fused(n, cores, args):
+        return fused_layer(n, *args)
+    return per_device(*args)
+
+
 def solution(mesh):
     placed = (
         P(("groups", "ctx"), "exp"),
@@ -158,7 +558,7 @@
         P("ctx", None, None),
     )
     return jax.shard_map(
-        per_device,
+        layer,
         mesh=mesh,
         in_specs=placed,
         out_specs=P(("groups", "ctx"), "exp"),

time: 255 us -> 127 us (0.50)
  blocking collectives: 131 us -> 0 us
  Pallas kernels: 0 us -> 113 us
  waiting for transfers between devices: 61.1 us -> 0 us
  between operations: 13.6 us -> 0.02 us
  other arithmetic: 12.8 us -> 0 us
  matrix products: 10.4 us -> 0 us
  local copies, waits for them, and re-layouts: 20.3 us -> 11.3 us
  starting transfers between devices: 4.76 us -> 0 us
    pallas_call x0 -> x1, Pallas kernels: none -> 113 us  [fused_layer(): pl.pallas_call(functools.partial(layer_kernel, n), out_shape=jax.ShapeDty...]
    all_gather x2 -> x0, blocking collectives: 86.7 us -> none  [the longest x1 45.7 us: attend(): key_piece = lax.all_gather(key_rows, 'ctx', axis=0, tiled=True)]
    all_to_all x1 -> x0, blocking collectives: 44.7 us -> none  [per_device(): lax.all_to_all(own_slots, 'ctx', split_axis=0, concat_axis=0, tiled=True)]
    all_to_all x1 -> x0, waiting for transfers between devices: 32.8 us -> none  [per_device(): lax.all_to_all(partial_value, 'ctx', split_axis=0, concat_axis=0, tiled=T...]
    psum x1 -> x0, waiting for transfers between devices: 18.7 us -> none  [per_device(): lax.psum(head_part.astype(jnp.bfloat16), 'exp').astype(jnp.float32)]
    dot_general x5 -> x0, matrix products: 10.4 us -> none  [the longest x1 5.18 us: per_device(): jnp.einsum('sxmf,xfd->sxmd', hidden, w_down, preferred_element_type=jnp.f...]
    reduce_scatter x1 -> x0, waiting for transfers between devices: 9.5 us -> none  [per_device(): lax.psum_scatter(mixed_part.astype(jnp.bfloat16), 'exp', scatter_dimensio...]
    unnamed x17 -> x21, local copies, waits for them, and re-layouts: 2.58 us -> 11.3 us
  transfers between devices with their start and end apart: 3 -> 0, of which waited for: 3 -> 0; matrix products, arithmetic and copies ran while one was open for 2% -> 0% of each run, Pallas kernels for 0% -> 0%
where the time goes in v1:
time: 127 us; the launch traced here: 125 us
  Pallas kernels  113 us (89%)
  local copies, waits for them, and re-layouts  11.3 us (9%)
    pallas_call x1, Pallas kernels, fused_layer(): pl.pallas_call(functools.partial(layer_kernel, n), out_shape=jax.ShapeDty...  113 us
    unnamed x21, local copies, waits for them, and re-layouts  11.3 us

profile of v1, /device:TPU:0, one launch (start us, length us, event | category | flops | bytes accessed | tf_op | source)
XLA Modules:
  0.0 124.5 jit_solution(14665131731462410653)
XLA Ops:
  0.0 0.8 copy.12.ids_ref
  0.8 0.8 copy.13.gate_ref
  1.6 0.0 copy-start
  1.6 1.6 %copy-done = bf16[1024,1024]{1,0:T(8,128)(2,1)S(1)} copy-done((bf16[1024,1024]{1,0:T(8,128)(2,1)S(1)}, bf16[1024,1024]{1,0:T(8,128)(2,1)}, u32[]{:S(2)}) %copy-start) | copy-done | bytes 2097176
  3.2 0.0 copy-start.1
  3.2 1.1 copy-done.1
  4.3 0.0 copy-start.2
  4.3 1.1 copy-done.2
  5.4 0.0 copy-start.3
  5.4 1.1 copy-done.3
  6.6 0.0 copy-start.4
  6.6 0.9 copy-done.4
  7.5 0.0 copy-start.5
  7.5 0.9 copy-done.5
  8.5 0.0 copy-start.6
  8.5 0.8 copy-done.6
  9.2 0.0 copy-start.7
  9.2 0.8 copy-done.7
  10.0 0.0 copy-start.8
  10.0 0.7 copy-done.8
  10.7 113.2 %shard_map.109 = bf16[128,512]{1,0:T(8,128)(2,1)S(1)} custom-call(bf16[128,1024]{1,0:T(8,128)(2,1)S(1)} %copy-done.4, bf16[128,128]{1,0:T(8,128)(2,1)S(1)} %copy-done.6, bf16[128,128]{1,0:T(8,128)(2,1)S(1)} %copy-done.7, bf16[128,1024]{1,0:T(8,128)(2,1)S(1)} %copy-done.5, bf16[1024,1024]{1,0:T(8,128)(2,1)S(1)} %copy-done, f32[1,1024]{1,0:T(1,128)S(1)} %bitcast.1, ...), custom_call_target="tpu_custom_call" | custom-call | tf_op jit(solution)/shard_map/pallas_call | solution.py:497
  123.9 0.7 copy.15
Async XLA Ops:
  1.6 1.6 %copy-start = (bf16[1024,1024]{1,0:T(8,128)(2,1)S(1)}, bf16[1024,1024]{1,0:T(8,128)(2,1)}, u32[]{:S(2)}) copy-start(bf16[1024,1024]{1,0:T(8,128)(2,1)} %proj_hbm.1) | copy-start | bytes 6291460
  3.2 1.1 copy-start.1
  4.3 1.1 copy-start.2
  5.4 1.1 copy-start.3
  6.6 0.9 copy-start.4
  7.5 0.9 copy-start.5
  8.5 0.8 copy-start.6
  9.2 0.8 copy-start.7
  10.0 0.7 copy-start.8

commit v2 on v1

--- a/solution.py
+++ b/solution.py
@@ -10,9 +10,9 @@
 
 MESH = pl.DeviceIdType.MESH
 HEAD = 128
-PIECES = 2
+PIECES = 4
 NEG = -1e30
-STAGGER = 1
+STAGGER = 0
 
 
 def attend(queries, key_rows, value_rows, first):
@@ -171,7 +171,8 @@
     wd_hbm,
     out_ref,
     kv_buf,
-    co_buf,
+    co_out,
+    co_in,
     row_buf,
     con_buf,
     rs_bufs,
@@ -193,6 +194,7 @@
     load_sem,
     kv_sem,
     co_sem,
+    w_sem,
     ag_sem,
     rs_sem,
     half_sem,
@@ -210,41 +212,98 @@
     side = width // 2
     coord = [(me // 2 ** (bits - 1 - d)) % 2 for d in range(bits)]
     partner = [me + (1 - 2 * coord[d]) * 2 ** (bits - 1 - d) for d in range(bits)]
-    forward = list(range(bits))
-    crossed = forward[:-2] + [forward[-1], forward[-2]]
-    orders = [forward if p % 2 == 0 else crossed for p in range(PIECES)]
+    far, near, last = list(range(bits - 2)), bits - 2, bits - 1
+    kv_orders = [
+        far + [near, last],
+        far + [last, near],
+        [near, last] + far,
+        [last] + far + [near],
+    ]
+    orders = [far + [near], far + [near], far + [near], [near] + far]
+    places = n // 2
+    parity = coord[last]
     other = 1 - core
 
+    halves = [pl.ds(pl.multiple_of(core * (w.shape[1] // 2), 16), w.shape[1] // 2) for w in (wg, wu, wd)]
     loads = [
         pltpu.make_async_copy(src, dst, load_sem.at[i])
         for i, (src, dst) in enumerate(
-            [(proj_hbm, proj), (wg_hbm.at[0], wg), (wu_hbm.at[0], wu), (wd_hbm.at[0], wd)]
+            [
+                (proj_hbm, proj),
+                (wg_hbm.at[0], wg.at[parity]),
+                (wu_hbm.at[0], wu.at[parity]),
+                (wd_hbm.at[0], wd.at[parity]),
+            ]
         )
     ]
     for load in loads:
         load.start()
 
     barrier = pltpu.get_barrier_semaphore()
-    for d in range(bits):
+    for hop in range(1, n):
         pl.semaphore_signal(
-            barrier, inc=1, device_id=(group, partner[d], core), device_id_type=MESH
+            barrier, inc=1, device_id=(group, (me + hop) % n, core), device_id_type=MESH
         )
     pl.semaphore_signal(barrier, inc=1, device_id=(group, me, other), device_id_type=MESH)
 
     own = tuple(coord)
-    kv_buf[(0,) + own] = k_ref[...]
-    kv_buf[(1,) + own] = v_ref[...]
+    for i, ref in enumerate((k_ref, v_ref)):
+        kv_buf[(2 * i,) + own] = ref[:half, :]
+        kv_buf[(2 * i + 1,) + own] = ref[half:, :]
     mix = gate_ref[...] / jnp.sum(gate_ref[...], axis=1, keepdims=True)
     lane = lax.broadcasted_iota(jnp.int32, (rows, HEAD), 1)
     coef = jnp.zeros((rows, HEAD), jnp.float32)
     for k in range(ids_ref.shape[1]):
         coef = coef + jnp.where(ids_ref[:, k : k + 1] == lane, mix[:, k : k + 1], 0.0)
-    co_buf[own] = coef.T[: co_buf.shape[bits]]
-    pl.semaphore_wait(barrier, bits + 1)
+    by_expert = coef.T
+    co_out[...] = jnp.zeros(co_out.shape, jnp.float32)
+    for e in range(places):
+        co_out[e, :2, :] = by_expert[2 * e : 2 * e + 2, :]
+    pl.semaphore_wait(barrier, n)
+
+    def expert_copy(i):
+        return pltpu.make_async_remote_copy(
+            src_ref=(wg_hbm, wu_hbm, wd_hbm)[i].at[0, halves[i]],
+            dst_ref=(wg, wu, wd)[i].at[parity, halves[i]],
+            send_sem=w_sem.at[i, 0, 0],
+            recv_sem=w_sem.at[i, 0, 1],
+            device_id=(group, partner[last], core),
+            device_id_type=MESH,
+        )
+
+    def share_copy(i):
+        here = (wg, wu, wd)[i].at[1 - parity, halves[i]]
+        return pltpu.make_async_remote_copy(
+            src_ref=here,
+            dst_ref=here,
+            send_sem=w_sem.at[i, 1, 0],
+            recv_sem=w_sem.at[i, 1, 1],
+            device_id=(group, me, other),
+            device_id_type=MESH,
+        )
+
+    def share(i):
+        copy = expert_copy(i)
+        copy.wait_recv()
+        share_copy(i).start()
+        sent.extend([copy, share_copy(i)])
+
+    def weight_copy(hop):
+        to = (me + 2 * hop) % n
+        return pltpu.make_async_remote_copy(
+            src_ref=co_out.at[to // 2],
+            dst_ref=co_in.at[me // 2],
+            send_sem=co_sem.at[hop, 0],
+            recv_sem=co_sem.at[hop, 1],
+            device_id=(group, to, core),
+            device_id_type=MESH,
+        )
 
     def gather(buf, lead, order, step, sems):
         done = order[:step]
-        where = lead + tuple(slice(None) if d in done else coord[d] for d in range(bits))
+        where = lead + tuple(
+            slice(None) if d in done else coord[d] for d in range(len(order))
+        )
         return pltpu.make_async_remote_copy(
             src_ref=buf.at[where],
             dst_ref=buf.at[where],
@@ -256,46 +315,48 @@
 
     sent = []
 
-    def kv_copies(step):
-        copies = [
-            gather(
-                kv_buf,
-                (i,),
-                [forward, crossed][i],
-                step,
-                (kv_sem.at[i, step, 0], kv_sem.at[i, step, 1]),
-            )
-            for i in range(2)
-        ]
-        copies.append(
-            gather(co_buf, (), forward, step, (co_sem.at[step, 0], co_sem.at[step, 1]))
-        )
-        return copies
-
+    def kv_copy(i, step):
+        return gather(
+            kv_buf, (i,), kv_orders[i], step, (kv_sem.at[i, step, 0], kv_sem.at[i, step, 1])
+        )
+
+    for i in range(4):
+        kv_copy(i, 0).start()
+    for hop in range(1, places):
+        copy = weight_copy(hop)
+        copy.start()
+        sent.append(copy)
+    for h in range(heads):
+        queries[h] = q_ref[:, h * HEAD : (h + 1) * HEAD]
+    top[...] = jnp.full(top.shape, NEG, jnp.float32)
+    den[...] = jnp.zeros(den.shape, jnp.float32)
+    acc[...] = jnp.zeros(acc.shape, jnp.float32)
     for step in range(bits):
-        copies = kv_copies(step)
-        for copy in copies:
-            copy.start()
-        if step == 0:
-            for h in range(heads):
-                queries[h] = q_ref[:, h * HEAD : (h + 1) * HEAD]
-            top[...] = jnp.full(top.shape, NEG, jnp.float32)
-            den[...] = jnp.zeros(den.shape, jnp.float32)
-            acc[...] = jnp.zeros(acc.shape, jnp.float32)
-        for copy in copies:
+        for i in range(4):
+            copy = kv_copy(i, step)
             copy.wait_recv()
-        sent += copies
+            sent.append(copy)
+            if step < bits - 1:
+                kv_copy(i, step + 1).start()
+
+    for i in range(3):
+        expert_copy(i).start()
 
     span = 4 * rows
     chunk = me // 4
     unit = HEAD ** (-0.5) * math.log2(math.e)
     row_pos = lax.broadcasted_iota(jnp.int32, (rows, span), 0) + (me % 4) * rows
-    col_pos = lax.broadcasted_iota(jnp.int32, (rows, span), 1)
+    column = lax.broadcasted_iota(jnp.int32, (rows, span), 1)
+    col_pos = (column % (2 * rows)) // half * rows + column // (2 * rows) * half + column % half
 
     def attend_chunk(j, carry):
         at = tuple((j // 2 ** (bits - 3 - d)) % 2 for d in range(bits - 2))
-        keys = kv_buf[(0,) + at].reshape(span, HEAD)
-        values = kv_buf[(1,) + at].reshape(span, HEAD)
+        keys, values = (
+            jnp.concatenate(
+                [kv_buf[(i,) + at].reshape(2 * rows, HEAD) for i in pair], axis=0
+            )
+            for pair in ((0, 1), (2, 3))
+        )
         allowed = col_pos <= row_pos + (chunk - j) * span
         for h in range(heads):
             scores = lax.dot_general(
@@ -338,9 +399,12 @@
         att[mine, :], proj[...], preferred_element_type=jnp.float32
     )
     by_token[...] = jnp.zeros(by_token.shape, jnp.float32)
-    for b in range(n):
-        at = tuple((b // 2 ** (bits - 1 - d)) % 2 for d in range(bits))
-        by_token[b : b + 1, :] = co_buf[at + (pl.ds(me, 1), slice(None))]
+    co_in[me // 2] = co_out[me // 2]
+    for hop in range(1, places):
+        weight_copy(hop).wait_recv()
+    for b in range(places):
+        for j in range(2):
+            by_token[j * places + b : j * places + b + 1, :] = co_in[b, j : j + 1, :]
     by_token[...] = by_token[...].T
     swap.wait_recv()
     sent.append(swap)
@@ -360,7 +424,7 @@
         turn = order[step]
         where = (p,) + tuple(
             coord[d] if d in done else (1 - coord[d] if d == turn else slice(None))
-            for d in range(bits)
+            for d in range(bits - 1)
         )
         return pltpu.make_async_remote_copy(
             src_ref=con_buf.at[where],
@@ -383,48 +447,54 @@
 
     def experts(p):
         if p == 0:
+            share(2)
             for load in loads[1:]:
                 load.wait()
-        count = n * piece_rows
-        x = row_buf[p].reshape(count, width)
-        gate = jnp.dot(x, wg[...], preferred_element_type=jnp.float32)
-        upper = jnp.dot(x, wu[...], preferred_element_type=jnp.float32)
-        hidden = (gate / (1.0 + jnp.exp(-gate)) * upper).astype(jnp.bfloat16)
-        part = jnp.dot(hidden, wd[...], preferred_element_type=jnp.float32)
+            for i in range(3):
+                share_copy(i).wait_recv()
+        x = row_buf[p].reshape(places * piece_rows, width)
         first = pl.multiple_of(core * half + p * piece_rows, piece_rows)
         columns = by_token[pl.ds(first, piece_rows), :]
-        for b in range(n):
-            at = tuple((b // 2 ** (bits - 1 - d)) % 2 for d in range(bits))
+        parts = []
+        for j in range(2):
+            gate = jnp.dot(x, wg[j], preferred_element_type=jnp.float32)
+            upper = jnp.dot(x, wu[j], preferred_element_type=jnp.float32)
+            hidden = (gate / (1.0 + jnp.exp(-gate)) * upper).astype(jnp.bfloat16)
+            parts.append(jnp.dot(hidden, wd[j], preferred_element_type=jnp.float32))
+        for b in range(places):
+            at = tuple((b // 2 ** (bits - 2 - d)) % 2 for d in range(bits - 1))
+            some = slice(b * piece_rows, (b + 1) * piece_rows)
             con_buf[(p,) + at] = (
-                part[b * piece_rows : (b + 1) * piece_rows] * columns[:, b : b + 1]
+                parts[0][some] * columns[:, b : b + 1]
+                + parts[1][some] * columns[:, places + b : places + b + 1]
             ).astype(jnp.bfloat16)
 
     def stage(p, s):
         if s == 0:
-            row_buf[(p,) + own] = normed[p * piece_rows : (p + 1) * piece_rows]
+            row_buf[(p,) + own[:-1]] = normed[p * piece_rows : (p + 1) * piece_rows]
             row_copy(p, 0).start()
             return
-        if s <= bits:
+        if s < bits:
             copy = row_copy(p, s - 1)
             copy.wait_recv()
             sent.append(copy)
-            if s < bits:
+            if s < bits - 1:
                 row_copy(p, s).start()
                 return
             experts(p)
             rs_copy(p, 0).start()
             return
-        s -= bits + 1
-        if s < bits:
+        s -= bits
+        if s < bits - 1:
             copy = rs_copy(p, s)
             copy.wait_recv()
             sent.append(copy)
             order = orders[p][::-1]
             where = (p,) + tuple(
-                coord[d] if d in order[: s + 1] else slice(None) for d in range(bits)
+                coord[d] if d in order[: s + 1] else slice(None) for d in range(bits - 1)
             )
             total = con_buf[where].astype(jnp.float32) + rs_bufs[s][p].astype(jnp.float32)
-            if s < bits - 1:
+            if s < bits - 2:
                 con_buf[where] = total.astype(jnp.bfloat16)
                 rs_copy(p, s + 1).start()
                 return
@@ -442,9 +512,11 @@
         first = pl.multiple_of(other * half + p * piece_rows, piece_rows)
         out_ref[pl.ds(first, piece_rows), :] = fin_in[p]
 
-    stages = 2 * bits + 2
+    stages = 2 * bits
     plan = sorted((s + STAGGER * p, p, s) for p in range(PIECES) for s in range(stages))
     for _, p, s in plan:
+        if p == 0 and 1 <= s < 3:
+            share(s - 1)
         stage(p, s)
     for copy in sent:
         copy.wait_send()
@@ -463,13 +535,14 @@
     anywhere = pl.BlockSpec(memory_space=pl.ANY)
     bf16, f32 = jnp.bfloat16, jnp.float32
     scratch = [
-        pltpu.VMEM((2,) + cube + (rows, HEAD), bf16),
-        pltpu.VMEM(cube + (-(-n // 8) * 8, rows), f32),
-        pltpu.VMEM((PIECES,) + cube + (piece_rows, width), bf16),
-        pltpu.VMEM((PIECES,) + cube + (piece_rows, width), bf16),
+        pltpu.VMEM((4,) + cube + (half, HEAD), bf16),
+        pltpu.VMEM((n // 2, 8, rows), f32),
+        pltpu.VMEM((n // 2, 8, rows), f32),
+        pltpu.VMEM((PIECES,) + cube[1:] + (piece_rows, width), bf16),
+        pltpu.VMEM((PIECES,) + cube[1:] + (piece_rows, width), bf16),
         [
-            pltpu.VMEM((PIECES,) + cube[s + 1 :] + (piece_rows, width), bf16)
-            for s in range(bits)
+            pltpu.VMEM((PIECES,) + cube[s + 2 :] + (piece_rows, width), bf16)
+            for s in range(bits - 1)
         ],
         pltpu.VMEM((half, width), bf16),
         pltpu.VMEM((half, width), bf16),
@@ -483,14 +556,15 @@
         pltpu.VMEM((half, width), f32),
         pltpu.VMEM((rows, rows), f32),
         pltpu.VMEM(out_proj.shape, bf16),
-        pltpu.VMEM(w_gate.shape[1:], bf16),
-        pltpu.VMEM(w_up.shape[1:], bf16),
-        pltpu.VMEM(w_down.shape[1:], bf16),
+        pltpu.VMEM((2,) + w_gate.shape[1:], bf16),
+        pltpu.VMEM((2,) + w_up.shape[1:], bf16),
+        pltpu.VMEM((2,) + w_down.shape[1:], bf16),
         pltpu.SemaphoreType.DMA((4,)),
-        pltpu.SemaphoreType.DMA((2, bits, 2)),
-        pltpu.SemaphoreType.DMA((bits, 2)),
-        pltpu.SemaphoreType.DMA((PIECES, bits, 2)),
-        pltpu.SemaphoreType.DMA((PIECES, bits, 2)),
+        pltpu.SemaphoreType.DMA((4, bits, 2)),
+        pltpu.SemaphoreType.DMA((n, 2)),
+        pltpu.SemaphoreType.DMA((3, 2, 2)),
+        pltpu.SemaphoreType.DMA((PIECES, bits - 1, 2)),
+        pltpu.SemaphoreType.DMA((PIECES, bits - 1, 2)),
         pltpu.SemaphoreType.DMA((2,)),
         pltpu.SemaphoreType.DMA((PIECES, 2)),
     ]
@@ -520,7 +594,7 @@
 
 def fits_fused(n, cores, args):
     queries, key_rows, hidden_in = args[0], args[1], args[3]
-    expert_ids, w_gate = args[6], args[8]
+    expert_ids, w_gate, w_down = args[6], args[8], args[10]
     rows, width = hidden_in.shape
     return (
         cores == 2
@@ -528,6 +602,8 @@
         and n & (n - 1) == 0
         and n <= HEAD
         and w_gate.shape[0] == 1
+        and w_gate.shape[1] % 32 == 0
+        and w_down.shape[1] % 32 == 0
         and 2 * expert_ids.shape[1] >= n
         and key_rows.shape[1] == HEAD
         and rows == HEAD

time: 127 us -> 84.8 us (0.67); the launches traced: 125 us -> 84.2 us
  Pallas kernels: 113 us -> 72.9 us
    pallas_call x1, Pallas kernels: 113 us -> 72.9 us  [fused_layer(): pl.pallas_call(functools.partial(layer_kernel, n), out_shape=jax.ShapeDty...]
where the time goes in v2:
time: 84.8 us; the launch traced here: 84.2 us
  Pallas kernels  72.9 us (86%)
  local copies, waits for them, and re-layouts  11.3 us (13%)
    pallas_call x1, Pallas kernels, fused_layer(): pl.pallas_call(functools.partial(layer_kernel, n), out_shape=jax.ShapeDty...  72.9 us
    unnamed x21, local copies, waits for them, and re-layouts  11.3 us

profile of v2, /device:TPU:0, one launch (start us, length us, event | category | flops | bytes accessed | tf_op | source)
XLA Modules:
  0.0 84.2 jit_solution(11184711988653943883)
XLA Ops:
  0.0 0.8 copy.12.ids_ref
  0.8 0.8 copy.13.gate_ref
  1.6 0.0 copy-start
  1.6 1.6 %copy-done = bf16[1024,1024]{1,0:T(8,128)(2,1)S(1)} copy-done((bf16[1024,1024]{1,0:T(8,128)(2,1)S(1)}, bf16[1024,1024]{1,0:T(8,128)(2,1)}, u32[]{:S(2)}) %copy-start) | copy-done | bytes 2097176
  3.2 0.0 copy-start.1
  3.2 1.1 %copy-done.1 = bf16[1,1024,384]{2,1,0:T(8,128)(2,1)S(1)} copy-done((bf16[1,1024,384]{2,1,0:T(8,128)(2,1)S(1)}, bf16[1,1024,384]{2,1,0:T(8,128)(2,1)}, u32[]{:S(2)}) %copy-start.1) | copy-done | bytes 786456
  4.3 0.0 copy-start.2
  4.3 1.1 %copy-done.2 = bf16[1,1024,384]{2,1,0:T(8,128)(2,1)S(1)} copy-done((bf16[1,1024,384]{2,1,0:T(8,128)(2,1)S(1)}, bf16[1,1024,384]{2,1,0:T(8,128)(2,1)}, u32[]{:S(2)}) %copy-start.2) | copy-done | bytes 786456
  5.4 0.0 copy-start.3
  5.4 1.1 %copy-done.3 = bf16[1,384,1024]{2,1,0:T(8,128)(2,1)S(1)} copy-done((bf16[1,384,1024]{2,1,0:T(8,128)(2,1)S(1)}, bf16[1,384,1024]{2,1,0:T(8,128)(2,1)}, u32[]{:S(2)}) %copy-start.3) | copy-done | bytes 786456
  6.6 0.0 copy-start.4
  6.6 0.9 %copy-done.4 = bf16[128,1024]{1,0:T(8,128)(2,1)S(1)} copy-done((bf16[128,1024]{1,0:T(8,128)(2,1)S(1)}, bf16[128,1024]{1,0:T(8,128)(2,1)}, u32[]{:S(2)}) %copy-start.4) | copy-done | bytes 262168
  7.5 0.0 copy-start.5
  7.5 0.9 %copy-done.5 = bf16[128,1024]{1,0:T(8,128)(2,1)S(1)} copy-done((bf16[128,1024]{1,0:T(8,128)(2,1)S(1)}, bf16[128,1024]{1,0:T(8,128)(2,1)}, u32[]{:S(2)}) %copy-start.5) | copy-done | bytes 262168
  8.5 0.0 copy-start.6
  8.5 0.8 copy-done.6
  9.2 0.0 copy-start.7
  9.2 0.8 copy-done.7
  10.0 0.0 copy-start.8
  10.0 0.7 copy-done.8
  10.7 72.9 %shard_map.109 = bf16[128,512]{1,0:T(8,128)(2,1)S(1)} custom-call(bf16[128,1024]{1,0:T(8,128)(2,1)S(1)} %copy-done.4, bf16[128,128]{1,0:T(8,128)(2,1)S(1)} %copy-done.6, bf16[128,128]{1,0:T(8,128)(2,1)S(1)} %copy-done.7, bf16[128,1024]{1,0:T(8,128)(2,1)S(1)} %copy-done.5, bf16[1024,1024]{1,0:T(8,128)(2,1)S(1)} %copy-done, f32[1,1024]{1,0:T(1,128)S(1)} %bitcast.1, ...), custom_call_target="tpu_custom_call" | custom-call | tf_op jit(solution)/shard_map/pallas_call | solution.py:571
  83.6 0.7 copy.15
Async XLA Ops:
  1.6 1.6 %copy-start = (bf16[1024,1024]{1,0:T(8,128)(2,1)S(1)}, bf16[1024,1024]{1,0:T(8,128)(2,1)}, u32[]{:S(2)}) copy-start(bf16[1024,1024]{1,0:T(8,128)(2,1)} %proj_hbm.1) | copy-start | bytes 6291460
  3.2 1.1 %copy-start.1 = (bf16[1,1024,384]{2,1,0:T(8,128)(2,1)S(1)}, bf16[1,1024,384]{2,1,0:T(8,128)(2,1)}, u32[]{:S(2)}) copy-start(bf16[1,1024,384]{2,1,0:T(8,128)(2,1)} %wg_hbm.1) | copy-start | bytes 2359300
  4.3 1.1 %copy-start.2 = (bf16[1,1024,384]{2,1,0:T(8,128)(2,1)S(1)}, bf16[1,1024,384]{2,1,0:T(8,128)(2,1)}, u32[]{:S(2)}) copy-start(bf16[1,1024,384]{2,1,0:T(8,128)(2,1)} %wu_hbm.1) | copy-start | bytes 2359300
  5.4 1.1 %copy-start.3 = (bf16[1,384,1024]{2,1,0:T(8,128)(2,1)S(1)}, bf16[1,384,1024]{2,1,0:T(8,128)(2,1)}, u32[]{:S(2)}) copy-start(bf16[1,384,1024]{2,1,0:T(8,128)(2,1)} %wd_hbm.1) | copy-start | bytes 2359300
  6.6 0.9 %copy-start.4 = (bf16[128,1024]{1,0:T(8,128)(2,1)S(1)}, bf16[128,1024]{1,0:T(8,128)(2,1)}, u32[]{:S(2)}) copy-start(bf16[128,1024]{1,0:T(8,128)(2,1)} %q_ref.1) | copy-start | bytes 786436
  7.5 0.9 %copy-start.5 = (bf16[128,1024]{1,0:T(8,128)(2,1)S(1)}, bf16[128,1024]{1,0:T(8,128)(2,1)}, u32[]{:S(2)}) copy-start(bf16[128,1024]{1,0:T(8,128)(2,1)} %hid_ref.1) | copy-start | bytes 786436
  8.5 0.8 copy-start.6
  9.2 0.8 copy-start.7
  10.0 0.7 copy-start.8
